TPU v7x, 32 devices: a whole 2x2x4 slice. The times are simulated.
32 devices in a mesh: row: 4 (over x, core), col: 8 (over z, y).
Axes of the slice: x: 2, y: 2, z: 4, core: 2. Of those that a mesh axis runs over, the one named last changes fastest.
Arguments:
- nodes: bfloat16 [2048, 512], P(('row', 'col')), may hold values from -6 to 6
- edges: bfloat16 [4, 8, 4096, 512], P('row', 'col'), may hold values from -6 to 6
- senders: int32 [4, 8, 4096], P('row', 'col'), may hold values from 0 to 255
- receivers: int32 [4, 8, 4096], P('row', 'col'), may hold values from 0 to 511
- levels: int32 [4, 8, 4096], P('row', 'col'), may hold values from 0 to 6
- counts: int32 [4, 8], P('row', 'col'), may hold values from 1 to 4096, as said below
- edge_w1: bfloat16 [3, 512, 512], replicated, may hold values from -0.15625 to 0.15625
- level_bias: bfloat16 [7, 512], replicated, may hold values from -6 to 6
- edge_w2: bfloat16 [512, 512], replicated, may hold values from -0.25 to 0.25
- edge_gain: float32 [512], replicated, may hold values from 0.1 to 1.9
- node_w1: bfloat16 [2, 512, 512], replicated, may hold values from -0.1875 to 0.1875
- node_w2: bfloat16 [512, 512], replicated, may hold values from -0.25 to 0.25
- node_gain: float32 [512], replicated, may hold values from 0.1 to 1.9
- grid: bfloat16 [32768, 512], P(('row', 'col')), may hold values from -6 to 6
- send_rows: int32 [32, 32, 4], P(('row', 'col')), may hold values from 0 to 63, as said below
- dec_index: int32 [32768, 3], P(('row', 'col')), may hold values from 0 to 127, as said below
- dec_w1: bfloat16 [2, 512, 512], replicated, may hold values from -0.1875 to 0.1875
- dec_w2: bfloat16 [512, 512], replicated, may hold values from -0.25 to 0.25
- dec_gain: float32 [512], replicated, may hold values from 0.1 to 1.9
Outputs:
- nodes_out: bfloat16 [2048, 512], P(('row', 'col'))
- edges_out: bfloat16 [4, 8, 4096, 512], P('row', 'col')
- grid_out: bfloat16 [32768, 512], P(('row', 'col'))
Inputs may be any that keep to these rules, and one draw needn't show every extreme that they name: `senders`: at slots at or beyond the tile's count the index is arbitrary and unused. `receivers`: at slots at or beyond the tile's count the index is arbitrary and unused. `counts`: some tile is full in every draw. `send_rows`: the 4 rows that one device sends to one band device are distinct. `dec_index`: buffer rows are laid out by source device, then slot; every row of a band's buffer is named by some decoder edge of that band.
All inputs are finite; a program needn't handle non-finite values.
Results may differ from a plain program's by a relative error of at most 0.015.
Values may be sent and summed in bfloat16 or wider, within the bound.
A program may use at most 128 MiB of HBM per device.

v0:
```python
import math

import jax
import jax.numpy as jnp
from jax import lax
from jax.sharding import PartitionSpec as P

EPSILON = 1e-05


def layer_norm(values, gain):
    center = values - jnp.mean(values, axis=-1, keepdims=True)
    spread = jnp.mean(center * center, axis=-1, keepdims=True)
    return center * lax.rsqrt(spread + EPSILON) * gain


def mlp_tail(pre, second_weight, gain):
    hidden = jax.nn.silu(pre).astype(jnp.bfloat16)
    output = jnp.dot(hidden, second_weight, preferred_element_type=jnp.float32)
    return layer_norm(output, gain)


def one_hot_rows(ids, count):
    return (ids[:, None] == jnp.arange(count, dtype=jnp.int32)[None, :]).astype(jnp.bfloat16)


def select_low(table_hot, table):
    return jnp.dot(table_hot, table, preferred_element_type=jnp.float32).astype(jnp.bfloat16)


def on_device(
    nodes,
    edges,
    senders,
    receivers,
    levels,
    counts,
    edge_w1,
    level_bias,
    edge_w2,
    edge_gain,
    node_w1,
    node_w2,
    node_gain,
    grid,
    send_rows,
    dec_index,
    dec_w1,
    dec_w2,
    dec_gain,
):
    node_block = nodes.shape[0]
    width = nodes.shape[1]
    capacity = edges.shape[2]
    level_count = level_bias.shape[0]
    sender_count = node_block * lax.axis_size("row")
    receiver_count = node_block * lax.axis_size("col")
    sender_block = lax.all_gather(nodes, "row", axis=0, tiled=True)
    receiver_block = lax.all_gather(nodes, "col", axis=0, tiled=True)
    joined_weight = edge_w1.reshape(3 * width, width)

    def first_layer(rows, send_hot, recv_hot):
        joined = jnp.concatenate(
            [rows, select_low(send_hot, sender_block), select_low(recv_hot, receiver_block)], axis=1
        )
        return jnp.dot(joined, joined_weight, preferred_element_type=jnp.float32)

    block_rows = math.gcd(capacity, 1024)
    block_count = capacity // block_rows
    slot_used = jnp.arange(capacity, dtype=jnp.int32) < counts[0, 0]
    items = (
        edges[0, 0].reshape(block_count, block_rows, width),
        senders[0, 0].reshape(block_count, block_rows),
        receivers[0, 0].reshape(block_count, block_rows),
        levels[0, 0].reshape(block_count, block_rows),
        slot_used.reshape(block_count, block_rows),
    )

    def edge_block(partial_value, item):
        rows, send_ids, recv_ids, level_ids, used = item
        send_hot = one_hot_rows(send_ids, sender_count)
        recv_hot = one_hot_rows(recv_ids, receiver_count)
        pre = first_layer(rows, send_hot, recv_hot)
        pre = pre + jnp.dot(
            one_hot_rows(level_ids, level_count), level_bias, preferred_element_type=jnp.float32
        )
        message = mlp_tail(pre, edge_w2, edge_gain).astype(jnp.bfloat16)
        kept = jnp.where(used[:, None], message, jnp.zeros((), jnp.bfloat16))
        updated = (rows.astype(jnp.float32) + kept.astype(jnp.float32)).astype(jnp.bfloat16)
        partial_value = partial_value + lax.dot_general(
            recv_hot, kept, (((0,), (0,)), ((), ())), preferred_element_type=jnp.float32
        )
        return (partial_value, updated)

    partial_value, edge_new = lax.scan(
        edge_block, jnp.zeros((receiver_count, width), jnp.float32), items
    )
    edges_out = edge_new.reshape(1, 1, capacity, width)
    summed = lax.psum(partial_value.astype(jnp.bfloat16), "col").astype(jnp.float32)
    aggregated = lax.dynamic_slice_in_dim(summed, lax.axis_index("col") * node_block, node_block, 0)
    node_pre = jnp.dot(nodes, node_w1[0], preferred_element_type=jnp.float32)
    node_pre = node_pre + jnp.dot(
        aggregated.astype(jnp.bfloat16), node_w1[1], preferred_element_type=jnp.float32
    )
    nodes_out = (nodes.astype(jnp.float32) + mlp_tail(node_pre, node_w2, node_gain)).astype(
        jnp.bfloat16
    )
    peers = send_rows.shape[1]
    per_peer = send_rows.shape[2]
    picked = select_low(one_hot_rows(send_rows[0].reshape(-1), node_block), nodes_out).reshape(
        peers, per_peer, width
    )
    received = lax.all_to_all(picked, ("row", "col"), split_axis=0, concat_axis=0, tiled=True)
    cells = grid.shape[0]
    fan_count = dec_index.shape[1]
    chosen = select_low(
        one_hot_rows(dec_index.reshape(-1), peers * per_peer),
        received.reshape(peers * per_peer, width),
    )
    node_dec = jnp.dot(chosen, dec_w1[1], preferred_element_type=jnp.float32).reshape(
        cells, fan_count, width
    )
    grid_part = jnp.dot(grid, dec_w1[0], preferred_element_type=jnp.float32)
    dec_pre = grid_part[:, None, :] + node_dec
    messages = mlp_tail(dec_pre.reshape(cells * fan_count, width), dec_w2, dec_gain).reshape(
        cells, fan_count, width
    )
    grid_out = (grid.astype(jnp.float32) + jnp.sum(messages, axis=1)).astype(jnp.bfloat16)
    return (nodes_out, edges_out, grid_out)


def solution(mesh):
    return jax.shard_map(
        on_device,
        mesh=mesh,
        in_specs=(
            P(("row", "col"), None),
            P("row", "col", None, None),
            P("row", "col", None),
            P("row", "col", None),
            P("row", "col", None),
            P("row", "col"),
            P(),
            P(),
            P(),
            P(),
            P(),
            P(),
            P(),
            P(("row", "col"), None),
            P(("row", "col"), None, None),
            P(("row", "col"), None),
            P(),
            P(),
            P(),
        ),
        out_specs=(P(("row", "col"), None), P("row", "col", None, None), P(("row", "col"), None)),
        check_vma=False,
    )
```

profile of v0, /device:TPU:0, one launch (start us, length us, event | category | flops | bytes accessed | tf_op | source)
XLA Modules:
  0.0 307.5 jit_solution(2291975846039022881)
XLA Ops:
  7.2 7.5 %all_gather.6 = bf16[256,512]{1,0:T(8,128)(2,1)S(1)} all-gather(bf16[64,512]{1,0:T(8,128)(2,1)} %param.21), channel_id=1, replica_groups=mesh['row'=4,'col'=8] {'row'}, dimensions={0}, use_global_device_ids=true | all-gather | bytes 327680 | tf_op jit(solution)/shard_map/all_gather | solution.py:58
  14.8 32.1 %all_gather.7 = bf16[512,512]{1,0:T(8,128)(2,1)S(1)} all-gather(bf16[64,512]{1,0:T(8,128)(2,1)} %param.21), channel_id=1, replica_groups=mesh['row'=4,'col'=8] {'col'}, dimensions={0}, use_global_device_ids=true | all-gather | bytes 589824 | tf_op jit(solution)/shard_map/all_gather | solution.py:59
  52.6 92.4 %while.13 = (s32[]{:T(128)}, f32[512,512]{1,0:T(8,128)}, bf16[4,1024,512]{2,1,0:T(8,128)(2,1)}, s32[4,1024]{1,0:T(4,128)S(1)}, pred[4,1024]{1,0:T(4,128)(4,1)S(1...) while((s32[]{:T(128)}, f32[512,512]{1,0:T(8,128)}, ...), condition=%wide.region_3.4_spmd.clone, body=%wide.region_0.3_spmd.clone.sunk | while | flops 3522437120 | bytes 37625100 | solution.py:95
  59.0 5.2 %fusion.88 = f32[1024,512]{1,0:T(8,128)} fusion(bf16[1536,512]{1,0:T(8,128)(2,1)} %get-tuple-element.307, bf16[1024,512]{0,1:T(8,128)(2,1)} %fusion.87, bf16[1024,512]{0,1:T(8,128)(2,1)} %convolution_convert_fusion.4, bf16[1024,512]{0,1:T(8,128)(2,1)S(1)} %bitcast.64), kind=kOutput, calls=%fused_computation.clone.1 | convolution fusion | flops 1620049920 | bytes 6815744 | tf_op jit(solution)/shard_map/while/body/eval_jaxpr/dot_general | solution.py:66
  64.2 2.9 fusion.89
  81.2 5.2 %fusion.88 = f32[1024,512]{1,0:T(8,128)} fusion(bf16[1536,512]{1,0:T(8,128)(2,1)} %get-tuple-element.307, bf16[1024,512]{0,1:T(8,128)(2,1)} %fusion.87, bf16[1024,512]{0,1:T(8,128)(2,1)} %convolution_convert_fusion.4, bf16[1024,512]{0,1:T(8,128)(2,1)S(1)} %bitcast.64), kind=kOutput, calls=%fused_computation.clone.1 | convolution fusion | flops 1620049920 | bytes 6815744 | tf_op jit(solution)/shard_map/while/body/eval_jaxpr/dot_general | solution.py:66
  86.4 2.9 fusion.89
  92.4 3.3 %convolution_add_fusion.3 = f32[512,512]{1,0:T(8,128)} fusion(f32[512,512]{1,0:T(8,128)} %get-tuple-element.283, s32[1024]{0:T(1024)S(1)} %bitcast.68, pred[]{:T(512)S(6)} %compare.3, f32[1024,512]{0,1:T(8,128)S(1)} %get-tuple-element.264, f32[512]{0:T(512)S(1)} %copy-done.5, f32[1024]{0:T(1024)S(1)} %add_rsqrt_fusion.4, ...), kind=kOutput, calls=%fused_computation.15.clone.1 | convolution fusion | flops 541065216 | bytes 4209665 | tf_op jit(solution)/shard_map/while/body/eval_jaxpr/dot_general | solution.py:90
  104.6 5.2 %fusion.88 = f32[1024,512]{1,0:T(8,128)} fusion(bf16[1536,512]{1,0:T(8,128)(2,1)} %get-tuple-element.307, bf16[1024,512]{0,1:T(8,128)(2,1)} %fusion.87, bf16[1024,512]{0,1:T(8,128)(2,1)} %convolution_convert_fusion.4, bf16[1024,512]{0,1:T(8,128)(2,1)S(1)} %bitcast.64), kind=kOutput, calls=%fused_computation.clone.1 | convolution fusion | flops 1620049920 | bytes 6815744 | tf_op jit(solution)/shard_map/while/body/eval_jaxpr/dot_general | solution.py:66
  115.8 3.3 %convolution_add_fusion.3 = f32[512,512]{1,0:T(8,128)} fusion(f32[512,512]{1,0:T(8,128)} %get-tuple-element.283, s32[1024]{0:T(1024)S(1)} %bitcast.68, pred[]{:T(512)S(6)} %compare.3, f32[1024,512]{0,1:T(8,128)S(1)} %get-tuple-element.264, f32[512]{0:T(512)S(1)} %copy-done.5, f32[1024]{0:T(1024)S(1)} %add_rsqrt_fusion.4, ...), kind=kOutput, calls=%fused_computation.15.clone.1 | convolution fusion | flops 541065216 | bytes 4209665 | tf_op jit(solution)/shard_map/while/body/eval_jaxpr/dot_general | solution.py:90
  128.0 5.2 %fusion.88 = f32[1024,512]{1,0:T(8,128)} fusion(bf16[1536,512]{1,0:T(8,128)(2,1)} %get-tuple-element.307, bf16[1024,512]{0,1:T(8,128)(2,1)} %fusion.87, bf16[1024,512]{0,1:T(8,128)(2,1)} %convolution_convert_fusion.4, bf16[1024,512]{0,1:T(8,128)(2,1)S(1)} %bitcast.64), kind=kOutput, calls=%fused_computation.clone.1 | convolution fusion | flops 1620049920 | bytes 6815744 | tf_op jit(solution)/shard_map/while/body/eval_jaxpr/dot_general | solution.py:66
  133.2 2.9 fusion.89
  139.2 3.3 %convolution_add_fusion.3 = f32[512,512]{1,0:T(8,128)} fusion(f32[512,512]{1,0:T(8,128)} %get-tuple-element.283, s32[1024]{0:T(1024)S(1)} %bitcast.68, pred[]{:T(512)S(6)} %compare.3, f32[1024,512]{0,1:T(8,128)S(1)} %get-tuple-element.264, f32[512]{0:T(512)S(1)} %copy-done.5, f32[1024]{0:T(1024)S(1)} %add_rsqrt_fusion.4, ...), kind=kOutput, calls=%fused_computation.15.clone.1 | convolution fusion | flops 541065216 | bytes 4209665 | tf_op jit(solution)/shard_map/while/body/eval_jaxpr/dot_general | solution.py:90
  148.2 72.3 %all-reduce.2.cloned.1.call-done = bf16[512,512]{1,0:T(8,128)(2,1)} async-done(((bf16[512,512]{1,0:T(8,128)(2,1)}), bf16[512,512]{1,0:T(8,128)(2,1)}) %all-reduce.2.cloned.1.call-update) | async-done | bytes 524304 | tf_op jit(solution)/shard_map/psum | solution.py:99
  223.1 4.1 %all-to-all-start = ((bf16[32,4,512]{2,1,0:T(4,128)(2,1)}), bf16[32,4,512]{2,1,0:T(4,128)(2,1)S(1)}, u32[]{:S(2)}, u32[]{:S(2)}) async-start(bf16[32,4,512]{2,1,0:T(4,128)(2,1)} %reshape.80), calls=%async_computation | async-start | bytes 262144 | tf_op jit(solution)/shard_map/all_to_all | solution.py:113
  229.2 5.5 %all-to-all-done = bf16[32,4,512]{2,1,0:T(4,128)(2,1)S(1)} async-done(((bf16[32,4,512]{2,1,0:T(4,128)(2,1)}), bf16[32,4,512]{2,1,0:T(4,128)(2,1)S(1)}, u32[]{:S(2)}, u32[]{:S(2)}) %all-to-all-start) | async-done | bytes 131104 | tf_op jit(solution)/shard_map/all_to_all | solution.py:113
  237.6 9.1 %dot_general.50 = bf16[1024,3,512]{2,1,0:T(4,128)(2,1)} reshape(bf16[3072,512]{1,0:T(8,128)(2,1)} %convolution_convert_fusion.1) | data formatting | bytes 6291456 | tf_op jit(solution)/shard_map/dot_general | solution.py:120
  246.7 4.4 %broadcast_add_fusion = f32[1024,3,512]{2,0,1:T(8,128)S(1)} fusion(f32[1024,512]{1,0:T(8,128)S(1)} %fusion.29, bf16[1024,3,512]{2,1,0:T(4,128)(2,1)} %dot_general.50, bf16[2,512,512]{2,1,0:T(8,128)(2,1)} %param.37), kind=kOutput, calls=%fused_computation.42 | convolution fusion | flops 1612185600 | bytes 13107200 | tf_op jit(solution)/shard_map/dot_general | solution.py:120
  251.2 7.5 %copy.30 = f32[1024,3,512]{2,1,0:T(4,128)} copy(f32[1024,3,512]{2,0,1:T(8,128)S(1)} %broadcast_add_fusion) | data formatting | bytes 12582912 | tf_op jit(solution)/shard_map/add | solution.py:124
  258.7 10.8 %reshape.82 = f32[3072,512]{1,0:T(8,128)} reshape(f32[1024,3,512]{2,1,0:T(4,128)} %copy.30) | data formatting | bytes 12582912 | tf_op jit(solution)/shard_map/reshape | solution.py:125
  269.5 4.2 %fusion.55 = (f32[3072]{0:T(1024)S(1)}, f32[3072,512]{1,0:T(8,128)S(1)}) fusion(bf16[512,512]{1,0:T(8,128)(2,1)S(1)} %copy-done, f32[3072,512]{1,0:T(8,128)} %reshape.82), kind=kOutput, calls=%fused_computation.78 | convolution fusion | flops 1620046848 | bytes 13119488 | tf_op jit(solution)/shard_map/dot_general | solution.py:19
  275.6 3.6 %multiply_multiply_fusion = f32[3072,512]{1,0:T(8,128)} fusion(f32[3072,512]{1,0:T(8,128)S(1)} %get-tuple-element.172, f32[512]{0:T(512)S(1)} %copy-done.8, f32[3072]{0:T(1024)S(1)} %add_rsqrt_fusion.1, f32[3072]{0:T(1024)S(1)} %broadcast_multiply_fusion.1), kind=kLoop, calls=%fused_computation.36 | loop fusion | flops 4718592 | bytes 12609536 | tf_op jit(solution)/shard_map/mul | solution.py:14
  279.2 10.5 %reshape.83 = f32[1024,3,512]{2,1,0:T(4,128)} reshape(f32[3072,512]{1,0:T(8,128)} %multiply_multiply_fusion) | data formatting | bytes 12582912 | tf_op jit(solution)/shard_map/reshape | solution.py:125
  289.7 8.4 %reduce_sum.67 = f32[1024,512]{1,0:T(8,128)S(1)} reduce(f32[1024,3,512]{2,1,0:T(4,128)} %reshape.83, f32[]{:T(128)} %constant.51.clone.1), dimensions={1}, to_apply=%region_9.10 | reduce | flops 1048576 | bytes 8388612 | tf_op jit(solution)/shard_map/reduce_sum | solution.py:128
  (128 shorter events, 72.8 us)
Async XLA Ops:
  7.2 262.3 %copy-start = (bf16[512,512]{1,0:T(8,128)(2,1)S(1)}, bf16[512,512]{1,0:T(8,128)(2,1)}, u32[]{:S(2)}) copy-start(bf16[512,512]{1,0:T(8,128)(2,1)} %param.38) | copy-start | bytes 1572868
  7.2 213.3 %all-reduce.2.cloned.1.call-start = ((), (), s32[]{:S(2)}) async-start(), calls=%async_computation.1 | async-start | bytes 1048576 | tf_op jit(solution)/shard_map/psum | solution.py:99
  52.6 94.7 %copy-start.9 = (s32[1,32,4]{1,2,0:T(4,128)S(1)}, s32[1,32,4]{1,2,0:T(4,128)}, u32[]{:S(2)}) copy-start(s32[1,32,4]{1,2,0:T(4,128)} %param.35) | copy-start | bytes 1540
  52.6 94.9 %copy-start.6 = (s32[1024,3]{0,1:T(4,128)S(1)}, s32[1024,3]{0,1:T(4,128)}, u32[]{:S(2)}) copy-start(s32[1024,3]{0,1:T(4,128)} %param.36) | copy-start | bytes 36868
  58.0 1.0 copy-start.1
  59.0 5.2 %copy-start.11 = (bf16[7,512]{1,0:T(8,128)(2,1)S(1)}, bf16[7,512]{1,0:T(8,128)(2,1)}, u32[]{:S(2)}) copy-start(bf16[7,512]{1,0:T(8,128)(2,1)} %get-tuple-element.309) | copy-start | bytes 21508 | tf_op jit(solution)/shard_map/while
  64.2 3.2 %copy-start.5 = (f32[512]{0:T(512)S(1)}, f32[512]{0:T(512)}, u32[]{:S(2)}) copy-start(f32[512]{0:T(512)} %get-tuple-element.311) | copy-start | bytes 6148 | tf_op jit(solution)/shard_map/while
  80.2 1.0 copy-start.1
  81.2 5.2 %copy-start.11 = (bf16[7,512]{1,0:T(8,128)(2,1)S(1)}, bf16[7,512]{1,0:T(8,128)(2,1)}, u32[]{:S(2)}) copy-start(bf16[7,512]{1,0:T(8,128)(2,1)} %get-tuple-element.309) | copy-start | bytes 21508 | tf_op jit(solution)/shard_map/while
  86.4 3.2 %copy-start.5 = (f32[512]{0:T(512)S(1)}, f32[512]{0:T(512)}, u32[]{:S(2)}) copy-start(f32[512]{0:T(512)} %get-tuple-element.311) | copy-start | bytes 6148 | tf_op jit(solution)/shard_map/while
  103.6 1.0 copy-start.1
  104.6 5.2 %copy-start.11 = (bf16[7,512]{1,0:T(8,128)(2,1)S(1)}, bf16[7,512]{1,0:T(8,128)(2,1)}, u32[]{:S(2)}) copy-start(bf16[7,512]{1,0:T(8,128)(2,1)} %get-tuple-element.309) | copy-start | bytes 21508 | tf_op jit(solution)/shard_map/while
  109.8 3.2 %copy-start.5 = (f32[512]{0:T(512)S(1)}, f32[512]{0:T(512)}, u32[]{:S(2)}) copy-start(f32[512]{0:T(512)} %get-tuple-element.311) | copy-start | bytes 6148 | tf_op jit(solution)/shard_map/while
  127.0 1.0 copy-start.1
  128.0 5.2 %copy-start.11 = (bf16[7,512]{1,0:T(8,128)(2,1)S(1)}, bf16[7,512]{1,0:T(8,128)(2,1)}, u32[]{:S(2)}) copy-start(bf16[7,512]{1,0:T(8,128)(2,1)} %get-tuple-element.309) | copy-start | bytes 21508 | tf_op jit(solution)/shard_map/while
  133.2 3.2 %copy-start.5 = (f32[512]{0:T(512)S(1)}, f32[512]{0:T(512)}, u32[]{:S(2)}) copy-start(f32[512]{0:T(512)} %get-tuple-element.311) | copy-start | bytes 6148 | tf_op jit(solution)/shard_map/while
  145.0 3.0 copy-start.2
  145.0 3.0 copy-start.3
  145.0 75.5 %copy-start.10 = (bf16[512,512]{1,0:T(8,128)(2,1)S(1)}, bf16[512,512]{1,0:T(8,128)(2,1)}, u32[]{:S(2)}) copy-start(bf16[512,512]{1,0:T(8,128)(2,1)} %param.32) | copy-start | bytes 1572868
  145.0 77.0 %copy-start.7 = (f32[512]{0:T(512)S(1)}, f32[512]{0:T(512)}, u32[]{:S(2)}) copy-start(f32[512]{0:T(512)} %param.33) | copy-start | bytes 6148
  222.2 15.5 %copy-start.4 = (bf16[64,512]{1,0:T(8,128)(2,1)}, bf16[64,512]{1,0:T(8,128)(2,1)S(1)}, u32[]{:S(2)}) copy-start(bf16[64,512]{1,0:T(8,128)(2,1)S(1)} %add_convert_fusion.2) | copy-start | bytes 196612
  223.1 11.6 %all-to-all-start = ((bf16[32,4,512]{2,1,0:T(4,128)(2,1)}), bf16[32,4,512]{2,1,0:T(4,128)(2,1)S(1)}, u32[]{:S(2)}, u32[]{:S(2)}) async-start(bf16[32,4,512]{2,1,0:T(4,128)(2,1)} %reshape.80), calls=%async_computation | async-start | bytes 262144 | tf_op jit(solution)/shard_map/all_to_all | solution.py:113
  273.6 2.0 copy-start.8
Sparse Core Ops, SparseCore 0:
  147.4 73.0 all-reduce.1
where the time goes:
time: 309 us; the launch traced here: 307 us
  waiting for transfers between devices  77.8 us (25%)
  matrix products  73.7 us (24%)
  local copies, waits for them, and re-layouts  61.6 us (20%)
  blocking collectives  39.7 us (13%)
  other arithmetic  35.4 us (11%)
  between operations  14.9 us (5%)
  starting transfers between devices  4.1 us (1%)
    psum x1, waiting for transfers between devices, on_device(): lax.psum(partial_value.astype(jnp.bfloat16), 'col').astype(jnp.float32)  72.3 us
    all_gather x1, blocking collectives, on_device(): receiver_block = lax.all_gather(nodes, 'col', axis=0, tiled=True)  32.1 us
    dot_general x4, matrix products, first_layer(): return jnp.dot(joined, joined_weight, preferred_element_type=jnp.float32)  20.9 us
    dot_general x6, matrix products, mlp_tail(): output = jnp.dot(hidden, second_weight, preferred_element_type=jnp.float32)  17.2 us
    dot_general x10, matrix products, select_low(): jnp.dot(table_hot, table, preferred_element_type=jnp.float32)  17 us
    dot_general x4, matrix products, edge_block(): lax.dot_general(recv_hot, kept, (((0,), (0,)), ((), ())), preferred_eleme...  12 us
    broadcast_in_dim x5, other arithmetic, on_device(): lax.scan(edge_block, jnp.zeros((receiver_count, width), jnp.float32), items)  10.8 us
    reshape x1, local copies, waits for them, and re-layouts, on_device(): dec_pre.reshape(cells * fan_count, width)  10.8 us
  transfers between devices with their start and end apart: 2, of which 2 were waited for; matrix products, arithmetic and copies ran while one was open for 1% of the time, Pallas kernels for 0%

commit v1 on v0

v1 whole, which is shorter than its diff:
```python
import functools
import math

import jax
import jax.numpy as jnp
from jax import lax
from jax.experimental import pallas as pl
from jax.experimental.pallas import tpu as pltpu
from jax.sharding import PartitionSpec as P

EPSILON = 1e-05
LANES = 128
MESH = pl.DeviceIdType.MESH
BF16 = jnp.bfloat16
F32 = jnp.float32
VMEM = pl.BlockSpec(memory_space=pltpu.VMEM)


def dot(left, right):
    return jnp.dot(left, right, preferred_element_type=F32)


def halved(weight):
    return (weight.astype(F32) * 0.5).astype(BF16)


def centred(weight):
    wide = weight.astype(F32)
    return (wide - jnp.mean(wide, axis=1, keepdims=True)).astype(BF16)


def silu_half(half):
    return (half + half * jnp.tanh(half)).astype(BF16)


def scaled(center, gain):
    spread = jnp.mean(center * center, axis=-1, keepdims=True)
    return center * lax.rsqrt(spread + EPSILON) * gain


def columns_of(rows):
    count = rows[0].shape[1]
    place = lax.broadcasted_iota(jnp.int32, (8, count), 0)
    joined = jnp.broadcast_to(rows[-1], (8, count))
    for index in range(len(rows) - 1):
        joined = jnp.where(place == index, jnp.broadcast_to(rows[index], (8, count)), joined)
    return joined.T


def hot(column, count):
    shape = (column.shape[0], count)
    return (lax.broadcasted_iota(jnp.int32, shape, 1) == column).astype(F32).astype(BF16)


def gather_kernel(n_row, n_col, nodes_ref, out_ref, send_sem, recv_sem):
    row, col = lax.axis_index("row"), lax.axis_index("col")
    block = nodes_ref.shape[0]
    barrier = pltpu.get_barrier_semaphore()
    for k in range(1, n_row):
        pl.semaphore_signal(barrier, inc=1, device_id=(lax.rem(row + k, n_row), col), device_id_type=MESH)
    for k in range(1, n_col):
        pl.semaphore_signal(barrier, inc=1, device_id=(row, lax.rem(col + k, n_col)), device_id_type=MESH)
    pl.semaphore_wait(barrier, n_row + n_col - 2)

    def slot(index):
        return out_ref.at[pl.ds(pl.multiple_of(index * block, block), block)]

    copies = []
    for k in range(1, n_col):
        copies.append((slot(n_row + col), k, (row, lax.rem(col + k, n_col)), slot(n_row + lax.rem(col + n_col - k, n_col))))
    for k in range(1, n_row):
        copies.append((slot(row), n_col + k, (lax.rem(row + k, n_row), col), slot(lax.rem(row + n_row - k, n_row))))
    started = []
    for target, sem, device, arrival in copies:
        copy = pltpu.make_async_remote_copy(
            nodes_ref, target, send_sem.at[sem], recv_sem.at[sem], device_id=device, device_id_type=MESH
        )
        copy.start()
        started.append(
            pltpu.make_async_remote_copy(
                nodes_ref, arrival, send_sem.at[sem], recv_sem.at[sem], device_id=device, device_id_type=MESH
            )
        )
    own = nodes_ref[...]
    slot(row)[...] = own
    slot(n_row + col)[...] = own
    for copy in started:
        copy.wait()


def edge_kernel(
    sender_count,
    chunk,
    counts_ref,
    edges_ref,
    senders_ref,
    receivers_ref,
    levels_ref,
    gathered_ref,
    w1_ref,
    bias_ref,
    w2_ref,
    gain_ref,
    edges_out_ref,
    partial_ref,
    table_ref,
    first_ref,
    second_ref,
    message_ref,
    total_ref,
):
    step = pl.program_id(0)
    rows = edges_ref.shape[0]
    receiver_count = partial_ref.shape[0]
    known = sender_count + receiver_count

    @pl.when(step == 0)
    def _():
        first_ref[...] = halved(w1_ref[0])
        second_ref[...] = centred(w2_ref[...])
        table_ref[:sender_count] = dot(gathered_ref[:sender_count], halved(w1_ref[1])).astype(BF16)
        table_ref[sender_count:known] = dot(gathered_ref[sender_count:], halved(w1_ref[2])).astype(BF16)
        table_ref[known:] = jnp.zeros((table_ref.shape[0] - known, table_ref.shape[1]), BF16)
        table_ref[known : known + bias_ref.shape[0]] = halved(bias_ref[...])
        total_ref[...] = jnp.zeros_like(total_ref)

    count = counts_ref[0, 0]
    gain = gain_ref[...]
    for part in range(rows // chunk):
        span = pl.ds(part * chunk, chunk)
        ids = columns_of([senders_ref[:, span], receivers_ref[:, span], levels_ref[:, span]])
        chosen = jnp.concatenate(
            [hot(ids[:, 0:1], sender_count), hot(ids[:, 1:2], receiver_count), hot(ids[:, 2:3], LANES)], axis=1
        )
        values = edges_ref[span]
        half = dot(values, first_ref[...]) + dot(chosen, table_ref[...])
        message = scaled(dot(silu_half(half), second_ref[...]), gain).astype(BF16)
        message_ref[span] = message
        place = step * rows + part * chunk + lax.broadcasted_iota(jnp.int32, (chunk, 1), 0)
        kept = jnp.where(place < count, message.astype(F32), 0.0)
        edges_out_ref[span] = (values.astype(F32) + kept).astype(BF16)
    slots = step * rows + lax.broadcasted_iota(jnp.int32, (1, rows), 1)
    targets = jnp.where(slots < count, receivers_ref[...], -1)
    spread = (lax.broadcasted_iota(jnp.int32, (receiver_count, rows), 0) == targets).astype(F32).astype(BF16)
    total_ref[...] += dot(spread, message_ref[...])

    @pl.when(step == pl.num_programs(0) - 1)
    def _():
        partial_ref[...] = total_ref[...].astype(BF16)


def node_kernel(
    n_row,
    n_col,
    partial_ref,
    nodes_ref,
    w1_ref,
    w2_ref,
    gain_ref,
    rows_ref,
    nodes_out_ref,
    band_ref,
    landing_ref,
    picked_ref,
    sum_send,
    sum_recv,
    band_send,
    band_recv,
):
    row, col = lax.axis_index("row"), lax.axis_index("col")
    me = row * n_col + col
    n_dev = n_row * n_col
    block, width = nodes_ref.shape
    pieces = width // LANES
    per_peer = rows_ref.shape[1]
    tile = pieces * per_peer
    barrier = pltpu.get_barrier_semaphore()

    def device(index):
        return (index // n_col, lax.rem(index, n_col))

    def greet(k, carry):
        pl.semaphore_signal(barrier, inc=1, device_id=device(lax.rem(me + k, n_dev)), device_id_type=MESH)
        return carry

    lax.fori_loop(1, n_dev, greet, 0)
    pl.semaphore_wait(barrier, n_dev - 1)

    def sum_copy(k):
        other = lax.rem(col + k, n_col)
        return pltpu.make_async_remote_copy(
            partial_ref.at[pl.ds(pl.multiple_of(other * block, block), block)],
            landing_ref.at[k],
            sum_send.at[k],
            sum_recv.at[k],
            device_id=(row, other),
            device_id_type=MESH,
        )

    for k in range(1, n_col):
        sum_copy(k).start()
    base = dot(nodes_ref[...], halved(w1_ref[0]))
    lower = halved(w1_ref[1])
    second = centred(w2_ref[...])
    count = n_dev * tile
    owner = lax.broadcasted_iota(jnp.int32, (count, n_dev), 0) // tile
    spread = (owner == lax.broadcasted_iota(jnp.int32, (count, n_dev), 1)).astype(F32).astype(BF16)
    wanted = dot(spread, rows_ref[...].astype(F32).astype(BF16))
    which = lax.broadcasted_iota(jnp.int32, (count, per_peer), 0) % per_peer
    wanted = jnp.where(which == lax.broadcasted_iota(jnp.int32, (count, per_peer), 1), wanted, 0.0)
    wanted = jnp.sum(wanted, axis=1, keepdims=True)
    local = lax.broadcasted_iota(jnp.int32, (count, block), 1).astype(F32)
    select = (local == wanted).astype(F32).astype(BF16)
    piece_of = (lax.broadcasted_iota(jnp.int32, (count, LANES), 0) // per_peer) % pieces

    total = partial_ref[pl.ds(pl.multiple_of(col * block, block), block)].astype(F32)
    for k in range(1, n_col):
        sum_copy(k).wait()
        total = total + landing_ref[k].astype(F32)
    half = base + dot(total.astype(BF16), lower)
    fresh = scaled(dot(silu_half(half), second), gain_ref[...])
    fresh = (nodes_ref[...].astype(F32) + fresh).astype(BF16)
    nodes_out_ref[...] = fresh
    selected = jnp.zeros((count, LANES), F32)
    for c in range(pieces):
        selected = jnp.where(piece_of == c, dot(select, fresh[:, c * LANES : (c + 1) * LANES]), selected)
    picked_ref[...] = selected.astype(BF16)

    def part(ref, index):
        return ref.at[pl.ds(pl.multiple_of(index * tile, tile), tile)]

    def send(k, carry):
        other = lax.rem(me + k, n_dev)
        pltpu.make_async_remote_copy(
            part(picked_ref, other),
            part(band_ref, me),
            band_send.at[k],
            band_recv.at[k],
            device_id=device(other),
            device_id_type=MESH,
        ).start()
        return carry

    lax.fori_loop(1, n_dev, send, 0)
    part(band_ref, me)[...] = part(picked_ref, me)[...]

    def finish(k, carry):
        other = lax.rem(me + k, n_dev)
        source = lax.rem(me + n_dev - k, n_dev)
        pltpu.make_async_remote_copy(
            part(picked_ref, other),
            part(band_ref, source),
            band_send.at[k],
            band_recv.at[k],
            device_id=device(other),
            device_id_type=MESH,
        ).wait()
        return carry

    lax.fori_loop(1, n_dev, finish, 0)


def grid_kernel(
    per_peer, grid_ref, index_ref, band_ref, w1_ref, w2_ref, gain_ref, out_ref, first_ref, second_ref, table_ref
):
    count = table_ref.shape[0]
    pieces = grid_ref.shape[1] // LANES
    tile = pieces * per_peer

    @pl.when(pl.program_id(0) == 0)
    def _():
        first_ref[...] = halved(w1_ref[0])
        second_ref[...] = centred(w2_ref[...])
        shape = (count, count * pieces)
        sender = lax.broadcasted_iota(jnp.int32, shape, 0)
        start = sender // per_peer * tile + sender % per_peer
        place = lax.broadcasted_iota(jnp.int32, shape, 1)
        band = band_ref[...]
        table = jnp.zeros(table_ref.shape, F32)
        for c in range(pieces):
            order = (place == start + c * per_peer).astype(F32).astype(BF16)
            piece = dot(order, band).astype(BF16)
            table = table + dot(piece, halved(w1_ref[1, c * LANES : (c + 1) * LANES]))
        table_ref[...] = table.astype(BF16)

    values = grid_ref[...]
    gain = gain_ref[...]
    fan = index_ref.shape[0]
    ids = columns_of([index_ref[e : e + 1] for e in range(fan)])
    base = dot(values, first_ref[...])
    total = values.astype(F32)
    for e in range(fan):
        half = base + dot(hot(ids[:, e : e + 1], count), table_ref[...])
        total = total + scaled(dot(silu_half(half), second_ref[...]), gain)
    out_ref[...] = total.astype(BF16)


def whole(shape):
    return pl.BlockSpec(shape, lambda i: (0,) * len(shape))


def on_device(
    n_row,
    n_col,
    nodes,
    edges,
    senders,
    receivers,
    levels,
    counts,
    edge_w1,
    level_bias,
    edge_w2,
    edge_gain,
    node_w1,
    node_w2,
    node_gain,
    grid,
    send_rows,
    dec_index,
    dec_w1,
    dec_w2,
    dec_gain,
):
    block, width = nodes.shape
    capacity = edges.shape[2]
    n_dev = n_row * n_col
    sender_count, receiver_count = block * n_row, block * n_col
    known = sender_count + receiver_count

    gathered = pl.pallas_call(
        functools.partial(gather_kernel, n_row, n_col),
        out_shape=jax.ShapeDtypeStruct((known, width), BF16),
        in_specs=[VMEM],
        out_specs=VMEM,
        scratch_shapes=[pltpu.SemaphoreType.DMA((n_row + n_col,)), pltpu.SemaphoreType.DMA((n_row + n_col,))],
        compiler_params=pltpu.CompilerParams(
            collective_id=0, has_side_effects=True, vmem_limit_bytes=16 * 2**20
        ),
        name="gather_nodes",
    )(nodes)

    rows = math.gcd(capacity, 1024)
    chunk = math.gcd(rows, 256)
    table_rows = known + LANES

    def id_spec():
        return pl.BlockSpec((1, rows), lambda i: (0, i))

    edge_new, partial = pl.pallas_call(
        functools.partial(edge_kernel, sender_count, chunk),
        grid=(capacity // rows,),
        out_shape=(
            jax.ShapeDtypeStruct((capacity, width), BF16),
            jax.ShapeDtypeStruct((receiver_count, width), BF16),
        ),
        in_specs=[
            pl.BlockSpec(memory_space=pltpu.SMEM),
            pl.BlockSpec((rows, width), lambda i: (i, 0)),
            id_spec(),
            id_spec(),
            id_spec(),
            whole((known, width)),
            whole(edge_w1.shape),
            whole(level_bias.shape),
            whole(edge_w2.shape),
            whole((1, width)),
        ],
        out_specs=(pl.BlockSpec((rows, width), lambda i: (i, 0)), whole((receiver_count, width))),
        scratch_shapes=[
            pltpu.VMEM((table_rows, width), BF16),
            pltpu.VMEM((width, width), BF16),
            pltpu.VMEM((width, width), BF16),
            pltpu.VMEM((rows, width), BF16),
            pltpu.VMEM((receiver_count, width), F32),
        ],
        compiler_params=pltpu.CompilerParams(vmem_limit_bytes=44 * 2**20),
        name="edge_update",
    )(
        counts,
        edges.reshape(capacity, width),
        senders.reshape(1, capacity),
        receivers.reshape(1, capacity),
        levels.reshape(1, capacity),
        gathered,
        edge_w1,
        level_bias,
        edge_w2,
        edge_gain.reshape(1, width),
    )

    peers, per_peer = send_rows.shape[1:]
    tile = per_peer * (width // LANES)
    nodes_out, band = pl.pallas_call(
        functools.partial(node_kernel, n_row, n_col),
        out_shape=(
            jax.ShapeDtypeStruct((block, width), BF16),
            jax.ShapeDtypeStruct((peers * tile, LANES), BF16),
        ),
        in_specs=[VMEM] * 6,
        out_specs=(VMEM, VMEM),
        scratch_shapes=[
            pltpu.VMEM((n_col, block, width), BF16),
            pltpu.VMEM((peers * tile, LANES), BF16),
            pltpu.SemaphoreType.DMA((n_col,)),
            pltpu.SemaphoreType.DMA((n_col,)),
            pltpu.SemaphoreType.DMA((n_dev,)),
            pltpu.SemaphoreType.DMA((n_dev,)),
        ],
        compiler_params=pltpu.CompilerParams(
            collective_id=1, has_side_effects=True, vmem_limit_bytes=24 * 2**20
        ),
        name="node_update",
    )(partial, nodes, node_w1, node_w2, node_gain.reshape(1, width), send_rows.reshape(peers, per_peer))

    cells, fan = dec_index.shape
    cell_rows = math.gcd(cells, 256)
    grid_out = pl.pallas_call(
        functools.partial(grid_kernel, per_peer),
        grid=(cells // cell_rows,),
        out_shape=jax.ShapeDtypeStruct((cells, width), BF16),
        in_specs=[
            pl.BlockSpec((cell_rows, width), lambda i: (i, 0)),
            pl.BlockSpec((fan, cell_rows), lambda i: (0, i)),
            whole((peers * tile, LANES)),
            whole(dec_w1.shape),
            whole(dec_w2.shape),
            whole((1, width)),
        ],
        out_specs=pl.BlockSpec((cell_rows, width), lambda i: (i, 0)),
        scratch_shapes=[
            pltpu.VMEM((width, width), BF16),
            pltpu.VMEM((width, width), BF16),
            pltpu.VMEM((peers * per_peer, width), BF16),
        ],
        compiler_params=pltpu.CompilerParams(vmem_limit_bytes=40 * 2**20),
        name="grid_update",
    )(grid, dec_index.T, band, dec_w1, dec_w2, dec_gain.reshape(1, width))
    return (nodes_out, edge_new.reshape(edges.shape), grid_out)


def solution(mesh):
    return jax.shard_map(
        functools.partial(on_device, mesh.shape["row"], mesh.shape["col"]),
        mesh=mesh,
        in_specs=(
            P(("row", "col"), None),
            P("row", "col", None, None),
            P("row", "col", None),
            P("row", "col", None),
            P("row", "col", None),
            P("row", "col"),
            P(),
            P(),
            P(),
            P(),
            P(),
            P(),
            P(),
            P(("row", "col"), None),
            P(("row", "col"), None, None),
            P(("row", "col"), None),
            P(),
            P(),
            P(),
        ),
        out_specs=(P(("row", "col"), None), P("row", "col", None, None), P(("row", "col"), None)),
        check_vma=False,
    )
```

time: 309 us -> 84.7 us (0.27)
  waiting for transfers between devices: 77.8 us -> 0 us
  matrix products: 73.7 us -> 0 us
  Pallas kernels: 0 us -> 69 us
  local copies, waits for them, and re-layouts: 61.6 us -> 13.6 us
  blocking collectives: 39.7 us -> 0 us
  other arithmetic: 35.4 us -> 0 us
  between operations: 14.9 us -> 1.39 us
  starting transfers between devices: 4.1 us -> 0 us
    dot_general x27 -> x0, matrix products: 73.7 us -> none  [the longest x4 20.9 us: first_layer(): return jnp.dot(joined, joined_weight, preferred_element_type=jnp.float32)]
    psum x1 -> x0, waiting for transfers between devices: 72.3 us -> none  [on_device(): lax.psum(partial_value.astype(jnp.bfloat16), 'col').astype(jnp.float32)]
    pallas_call x0 -> x4, Pallas kernels: none -> 69 us  [the longest x1 28.8 us: on_device(): pl.pallas_call(functools.partial(node_kernel, n_row, n_col), out_shape=(j...]
    all_gather x2 -> x0, blocking collectives: 39.7 us -> none  [the longest x1 32.1 us: on_device(): receiver_block = lax.all_gather(nodes, 'col', axis=0, tiled=True)]
    reshape x4 -> x1, local copies, waits for them, and re-layouts: 22 us -> 0.09 us  [on_device(): send_rows.reshape(peers, per_peer)]
    unnamed x21 -> x43, local copies, waits for them, and re-layouts: 0.95 us -> 13.6 us
    reduce_sum x7 -> x0, other arithmetic: 11.7 us -> none  [the longest x1 8.37 us: on_device(): jnp.sum(messages, axis=1)]
    broadcast_in_dim x5 -> x0, other arithmetic: 10.8 us -> none  [on_device(): lax.scan(edge_block, jnp.zeros((receiver_count, width), jnp.float32), items)]
  transfers between devices with their start and end apart: 2 -> 0, of which waited for: 2 -> 0; matrix products, arithmetic and copies ran while one was open for 1% -> 0% of each run, Pallas kernels for 0% -> 0%
where the time goes in v1:
time: 84.7 us; the launch traced here: 84 us
  Pallas kernels  69 us (81%)
  local copies, waits for them, and re-layouts  13.6 us (16%)
  between operations  1.39 us (2%)
    pallas_call x1, Pallas kernels, on_device(): pl.pallas_call(functools.partial(node_kernel, n_row, n_col), out_shape=(j...  28.8 us
    pallas_call x1, Pallas kernels, on_device(): pl.pallas_call(functools.partial(edge_kernel, sender_count, chunk), grid=...  16.8 us
    pallas_call x1, Pallas kernels, on_device(): pl.pallas_call(functools.partial(gather_kernel, n_row, n_col), out_shape=...  15.5 us
    unnamed x43, local copies, waits for them, and re-layouts  13.6 us
    pallas_call x1, Pallas kernels, on_device(): pl.pallas_call(functools.partial(grid_kernel, per_peer), grid=(cells // c...  7.84 us

profile of v1, /device:TPU:0, one launch (start us, length us, event | category | flops | bytes accessed | tf_op | source)
XLA Modules:
  0.0 84.0 jit_solution(8864771189564840126)
XLA Ops:
  0.6 0.0 copy-start.10
  0.6 0.8 copy-done.10
  1.5 15.5 %gather_nodes.1.gathered_ref = bf16[768,512]{1,0:T(8,128)(2,1)S(1)} custom-call(bf16[64,512]{1,0:T(8,128)(2,1)S(1)} %copy-done.10), custom_call_target="tpu_custom_call" | custom-call | tf_op jit(solution)/shard_map/gather_nodes/pallas_call | solution.py:331
  17.6 0.0 copy-start
  17.6 2.2 %copy-done = bf16[1,1,4096,512]{3,2,1,0:T(8,128)(2,1)S(1)} copy-done((bf16[1,1,4096,512]{3,2,1,0:T(8,128)(2,1)S(1)}, bf16[1,1,4096,512]{3,2,1,0:T(8,128)(2,1)}, u32[]{:S(2)}) %copy-start) | copy-done | bytes 4194328
  19.8 1.4 %copy-done.1 = bf16[3,512,512]{2,1,0:T(8,128)(2,1)S(1)} copy-done((bf16[3,512,512]{2,1,0:T(8,128)(2,1)S(1)}, bf16[3,512,512]{2,1,0:T(8,128)(2,1)}, u32[]{:S(2)}) %copy-start.1) | copy-done | bytes 1572888
  21.2 1.0 %copy-done.5 = bf16[512,512]{1,0:T(8,128)(2,1)S(1)} copy-done((bf16[512,512]{1,0:T(8,128)(2,1)S(1)}, bf16[512,512]{1,0:T(8,128)(2,1)}, u32[]{:S(2)}) %copy-start.5) | copy-done | bytes 524312
  22.2 0.7 copy-done.12
  23.0 0.7 copy-done.13
  23.7 0.7 copy-done.14
  24.4 0.7 copy-done.16
  25.1 0.7 copy-done.18
  25.8 0.0 copy-start.17
  25.8 16.8 %edge_update.1 = (bf16[4096,512]{1,0:T(8,128)(2,1)}, bf16[512,512]{1,0:T(8,128)(2,1)S(1)}) custom-call(s32[1,1]{1,0:T(1,128)S(6)} %copy.24.counts_ref, bf16[4096,512]{1,0:T(8,128)(2,1)S(1)} %bitcast.10, s32[1,4096]{1,0:T(1,128)S(1)} %bitcast.11, s32[1,4096]{1,0:T(1,128)S(1)} %bitcast.12, s32[1,4096]{1,0:T(1,128)S(1)} %bitcast.13, ...), custom_call_target="tpu_custom_call" | custom-call | tf_op jit(solution)/shard_map/edge_update/pallas_call | solution.py:350
  42.6 0.8 copy-done.8
  43.4 0.1 copy.22.rows_ref
  43.5 0.0 copy-start.6
  43.5 1.0 %copy-done.6 = bf16[512,512]{1,0:T(8,128)(2,1)S(1)} copy-done((bf16[512,512]{1,0:T(8,128)(2,1)S(1)}, bf16[512,512]{1,0:T(8,128)(2,1)}, u32[]{:S(2)}) %copy-start.6) | copy-done | bytes 524312
  44.6 1.0 %copy-done.9 = bf16[512,512]{1,0:T(8,128)(2,1)S(1)} copy-done((bf16[512,512]{1,0:T(8,128)(2,1)S(1)}, bf16[512,512]{1,0:T(8,128)(2,1)}, u32[]{:S(2)}) %copy-start.9) | copy-done | bytes 524312
  45.6 28.8 %node_update.1 = (bf16[64,512]{1,0:T(8,128)(2,1)S(1)}, bf16[512,128]{1,0:T(8,128)(2,1)S(1)}) custom-call(bf16[512,512]{1,0:T(8,128)(2,1)S(1)} %copy-done.9, bf16[64,512]{1,0:T(8,128)(2,1)S(1)} %copy-done.11, bf16[2,512,512]{2,1,0:T(8,128)(2,1)S(1)} %copy-done.4, bf16[512,512]{1,0:T(8,128)(2,1)S(1)} %copy-done.6, f32[1,512]{1,0:T(1,128)S(1)} %bitcast.17, ...), custom_call_target="tpu_custom_call" | custom-call | tf_op jit(solution)/shard_map/node_update/pallas_call | solution.py:394
  74.5 0.0 copy-start.7
  74.5 1.0 %copy-done.7 = bf16[512,512]{1,0:T(8,128)(2,1)S(1)} copy-done((bf16[512,512]{1,0:T(8,128)(2,1)S(1)}, bf16[512,512]{1,0:T(8,128)(2,1)}, u32[]{:S(2)}) %copy-start.7) | copy-done | bytes 524312
  75.5 7.8 %grid_update.1 = bf16[1024,512]{1,0:T(8,128)(2,1)} custom-call(bf16[1024,512]{1,0:T(8,128)(2,1)S(1)} %copy-done.2, s32[3,1024]{1,0:T(4,128)S(1)} %bitcast.14, bf16[512,128]{1,0:T(8,128)(2,1)S(1)} %get-tuple-element.10.band_ref, bf16[2,512,512]{2,1,0:T(8,128)(2,1)S(1)} %copy-done.3, bf16[512,512]{1,0:T(8,128)(2,1)S(1)} %copy-done.7, f32[1,512]{1,0:T(1,128)S(1)} %bitcast.15), custom_call_target="tpu_custom_call" | custom-call | tf_op jit(solution)/shard_map/grid_update/pallas_call | solution.py:418
  83.4 0.6 copy.25
  (24 shorter events, 0.0 us)
Async XLA Ops:
  0.6 0.8 %copy-start.10 = (bf16[64,512]{1,0:T(8,128)(2,1)S(1)}, bf16[64,512]{1,0:T(8,128)(2,1)}, u32[]{:S(2)}) copy-start(bf16[64,512]{1,0:T(8,128)(2,1)} %nodes_ref.3) | copy-start | bytes 196612
  1.5 42.0 %copy-start.20 = (s32[1,32,4]{1,2,0:T(4,128)S(1)}, s32[1,32,4]{1,2,0:T(4,128)}, u32[]{:S(2)}) copy-start(s32[1,32,4]{1,2,0:T(4,128)} %param.33) | copy-start | bytes 1540
  1.5 42.0 %copy-start.11 = (bf16[64,512]{1,0:T(8,128)(2,1)S(1)}, bf16[64,512]{1,0:T(8,128)(2,1)}, u32[]{:S(2)}) copy-start(bf16[64,512]{1,0:T(8,128)(2,1)} %nodes_ref.3) | copy-start | bytes 196612
  1.5 42.0 %copy-start.19 = (f32[512]{0:T(512)S(1)}, f32[512]{0:T(512)}, u32[]{:S(2)}) copy-start(f32[512]{0:T(512)} %param.31) | copy-start | bytes 6148
  17.6 2.2 %copy-start = (bf16[1,1,4096,512]{3,2,1,0:T(8,128)(2,1)S(1)}, bf16[1,1,4096,512]{3,2,1,0:T(8,128)(2,1)}, u32[]{:S(2)}) copy-start(bf16[1,1,4096,512]{3,2,1,0:T(8,128)(2,1)} %param.20) | copy-start | bytes 12582916
  19.8 1.4 %copy-start.1 = (bf16[3,512,512]{2,1,0:T(8,128)(2,1)S(1)}, bf16[3,512,512]{2,1,0:T(8,128)(2,1)}, u32[]{:S(2)}) copy-start(bf16[3,512,512]{2,1,0:T(8,128)(2,1)} %w1_ref.3) | copy-start | bytes 4718596
  21.2 1.0 %copy-start.5 = (bf16[512,512]{1,0:T(8,128)(2,1)S(1)}, bf16[512,512]{1,0:T(8,128)(2,1)}, u32[]{:S(2)}) copy-start(bf16[512,512]{1,0:T(8,128)(2,1)} %w2_ref.3) | copy-start | bytes 1572868
  22.2 0.7 copy-start.12
  23.0 0.7 copy-start.13
  23.7 0.7 copy-start.14
  24.4 0.7 copy-start.16
  25.1 0.7 copy-start.18
  25.8 17.7 %copy-start.4 = (bf16[2,512,512]{2,1,0:T(8,128)(2,1)S(1)}, bf16[2,512,512]{2,1,0:T(8,128)(2,1)}, u32[]{:S(2)}) copy-start(bf16[2,512,512]{2,1,0:T(8,128)(2,1)} %w1_ref.4) | copy-start | bytes 3145732
  25.8 48.7 %copy-start.2 = (bf16[1024,512]{1,0:T(8,128)(2,1)S(1)}, bf16[1024,512]{1,0:T(8,128)(2,1)}, u32[]{:S(2)}) copy-start(bf16[1024,512]{1,0:T(8,128)(2,1)} %grid_ref.1) | copy-start | bytes 3145732
  25.8 48.7 %copy-start.3 = (bf16[2,512,512]{2,1,0:T(8,128)(2,1)S(1)}, bf16[2,512,512]{2,1,0:T(8,128)(2,1)}, u32[]{:S(2)}) copy-start(bf16[2,512,512]{2,1,0:T(8,128)(2,1)} %w1_ref.5) | copy-start | bytes 3145732
  25.8 48.7 %copy-start.15 = (s32[1024,3]{0,1:T(4,128)S(1)}, s32[1024,3]{0,1:T(4,128)}, u32[]{:S(2)}) copy-start(s32[1024,3]{0,1:T(4,128)} %param.34) | copy-start | bytes 36868
  25.8 48.7 %copy-start.17 = (f32[512]{0:T(512)S(1)}, f32[512]{0:T(512)}, u32[]{:S(2)}) copy-start(f32[512]{0:T(512)} %param.37) | copy-start | bytes 6148
  42.6 0.8 copy-start.8
  43.5 1.0 %copy-start.6 = (bf16[512,512]{1,0:T(8,128)(2,1)S(1)}, bf16[512,512]{1,0:T(8,128)(2,1)}, u32[]{:S(2)}) copy-start(bf16[512,512]{1,0:T(8,128)(2,1)} %w2_ref.4) | copy-start | bytes 1572868
  44.6 1.0 %copy-start.9 = (bf16[512,512]{1,0:T(8,128)(2,1)S(1)}, bf16[512,512]{1,0:T(8,128)(2,1)}, u32[]{:S(2)}) copy-start(bf16[512,512]{1,0:T(8,128)(2,1)} %copy-done.8) | copy-start | bytes 1572868
  74.5 1.0 %copy-start.7 = (bf16[512,512]{1,0:T(8,128)(2,1)S(1)}, bf16[512,512]{1,0:T(8,128)(2,1)}, u32[]{:S(2)}) copy-start(bf16[512,512]{1,0:T(8,128)(2,1)} %w2_ref.5) | copy-start | bytes 1572868

commit v2 on v1

--- a/solution.py
+++ b/solution.py
@@ -14,6 +14,8 @@
 BF16 = jnp.bfloat16
 F32 = jnp.float32
 VMEM = pl.BlockSpec(memory_space=pltpu.VMEM)
+ANY = pl.BlockSpec(memory_space=pl.ANY)
+VMEM_LIMIT = 60 * 2**20
 
 
 def dot(left, right):
@@ -52,40 +54,64 @@
     return (lax.broadcasted_iota(jnp.int32, shape, 1) == column).astype(F32).astype(BF16)
 
 
+def split_of(n_col):
+    outer = math.gcd(n_col, 4)
+    return outer, n_col // outer
+
+
 def gather_kernel(n_row, n_col, nodes_ref, out_ref, send_sem, recv_sem):
     row, col = lax.axis_index("row"), lax.axis_index("col")
+    outer, inner = split_of(n_col)
+    high, low = col // inner, lax.rem(col, inner)
     block = nodes_ref.shape[0]
+
+    def out_dev(k):
+        return (row, lax.rem(high + k, outer) * inner + low)
+
+    def in_dev(m):
+        return (row, high * inner + lax.rem(low + m, inner))
+
+    def row_dev(k):
+        return (lax.rem(row + k, n_row), col)
+
     barrier = pltpu.get_barrier_semaphore()
-    for k in range(1, n_row):
-        pl.semaphore_signal(barrier, inc=1, device_id=(lax.rem(row + k, n_row), col), device_id_type=MESH)
-    for k in range(1, n_col):
-        pl.semaphore_signal(barrier, inc=1, device_id=(row, lax.rem(col + k, n_col)), device_id_type=MESH)
-    pl.semaphore_wait(barrier, n_row + n_col - 2)
+    friends = [out_dev(k) for k in range(1, outer)] + [in_dev(m) for m in range(1, inner)]
+    friends += [row_dev(k) for k in range(1, n_row)]
+    for friend in friends:
+        pl.semaphore_signal(barrier, inc=1, device_id=friend, device_id_type=MESH)
+    pl.semaphore_wait(barrier, len(friends))
 
     def slot(index):
         return out_ref.at[pl.ds(pl.multiple_of(index * block, block), block)]
 
-    copies = []
-    for k in range(1, n_col):
-        copies.append((slot(n_row + col), k, (row, lax.rem(col + k, n_col)), slot(n_row + lax.rem(col + n_col - k, n_col))))
+    def col_slot(k, m):
+        return slot(n_row + lax.rem(high + outer - k, outer) * inner + lax.rem(low + inner - m, inner))
+
+    def copy(source, target, sem, device):
+        return pltpu.make_async_remote_copy(
+            source, target, send_sem.at[sem], recv_sem.at[sem], device_id=device, device_id_type=MESH
+        )
+
+    waits = []
+    for k in range(1, outer):
+        copy(nodes_ref, slot(n_row + col), k * inner, out_dev(k)).start()
+    for m in range(1, inner):
+        copy(nodes_ref, slot(n_row + col), m, in_dev(m)).start()
+        waits.append(copy(nodes_ref, col_slot(0, m), m, in_dev(m)))
     for k in range(1, n_row):
-        copies.append((slot(row), n_col + k, (lax.rem(row + k, n_row), col), slot(lax.rem(row + n_row - k, n_row))))
-    started = []
-    for target, sem, device, arrival in copies:
-        copy = pltpu.make_async_remote_copy(
-            nodes_ref, target, send_sem.at[sem], recv_sem.at[sem], device_id=device, device_id_type=MESH
-        )
-        copy.start()
-        started.append(
-            pltpu.make_async_remote_copy(
-                nodes_ref, arrival, send_sem.at[sem], recv_sem.at[sem], device_id=device, device_id_type=MESH
-            )
-        )
+        copy(nodes_ref, slot(row), n_col + k, row_dev(k)).start()
+        waits.append(copy(nodes_ref, slot(lax.rem(row + n_row - k, n_row)), n_col + k, row_dev(k)))
     own = nodes_ref[...]
     slot(row)[...] = own
     slot(n_row + col)[...] = own
-    for copy in started:
-        copy.wait()
+    for k in range(1, outer):
+        arrived = copy(nodes_ref, col_slot(k, 0), k * inner, out_dev(k))
+        arrived.wait()
+        for m in range(1, inner):
+            copy(col_slot(k, 0), col_slot(k, 0), k * inner + m, in_dev(m)).start()
+            waits.append(copy(col_slot(k, 0), col_slot(k, m), k * inner + m, in_dev(m)))
+    for wait in waits:
+        wait.wait()
 
 
 def edge_kernel(
@@ -154,20 +180,29 @@
     n_col,
     partial_ref,
     nodes_ref,
-    w1_ref,
-    w2_ref,
+    w1_hbm,
+    w2_hbm,
     gain_ref,
     rows_ref,
     nodes_out_ref,
     band_ref,
-    landing_ref,
+    w1_ref,
+    w2_ref,
+    near_ref,
+    stage_ref,
+    far_ref,
     picked_ref,
-    sum_send,
-    sum_recv,
+    load_sem,
+    near_send,
+    near_recv,
+    far_send,
+    far_recv,
     band_send,
     band_recv,
 ):
     row, col = lax.axis_index("row"), lax.axis_index("col")
+    outer, inner = split_of(n_col)
+    high, low = col // inner, lax.rem(col, inner)
     me = row * n_col + col
     n_dev = n_row * n_col
     block, width = nodes_ref.shape
@@ -184,24 +219,40 @@
         return carry
 
     lax.fori_loop(1, n_dev, greet, 0)
+    load_first = pltpu.make_async_copy(w1_hbm, w1_ref, load_sem.at[0])
+    load_second = pltpu.make_async_copy(w2_hbm, w2_ref, load_sem.at[1])
+    load_first.start()
+    load_second.start()
     pl.semaphore_wait(barrier, n_dev - 1)
 
-    def sum_copy(k):
-        other = lax.rem(col + k, n_col)
+    def sums(k, m):
+        index = lax.rem(high + k, outer) * inner + lax.rem(low + m, inner)
+        return partial_ref.at[pl.ds(pl.multiple_of(index * block, block), block)]
+
+    def near_copy(k, m):
         return pltpu.make_async_remote_copy(
-            partial_ref.at[pl.ds(pl.multiple_of(other * block, block), block)],
-            landing_ref.at[k],
-            sum_send.at[k],
-            sum_recv.at[k],
-            device_id=(row, other),
+            sums(k, m),
+            near_ref.at[k * inner + m],
+            near_send.at[k * inner + m],
+            near_recv.at[k * inner + m],
+            device_id=(row, high * inner + lax.rem(low + m, inner)),
             device_id_type=MESH,
         )
 
-    for k in range(1, n_col):
-        sum_copy(k).start()
-    base = dot(nodes_ref[...], halved(w1_ref[0]))
-    lower = halved(w1_ref[1])
-    second = centred(w2_ref[...])
+    def far_copy(k):
+        return pltpu.make_async_remote_copy(
+            stage_ref.at[k],
+            far_ref.at[k],
+            far_send.at[k],
+            far_recv.at[k],
+            device_id=(row, lax.rem(high + k, outer) * inner + low),
+            device_id_type=MESH,
+        )
+
+    order = list(range(1, outer)) + [0]
+    for k in order:
+        for m in range(1, inner):
+            near_copy(k, m).start()
     count = n_dev * tile
     owner = lax.broadcasted_iota(jnp.int32, (count, n_dev), 0) // tile
     spread = (owner == lax.broadcasted_iota(jnp.int32, (count, n_dev), 1)).astype(F32).astype(BF16)
@@ -213,10 +264,23 @@
     select = (local == wanted).astype(F32).astype(BF16)
     piece_of = (lax.broadcasted_iota(jnp.int32, (count, LANES), 0) // per_peer) % pieces
 
-    total = partial_ref[pl.ds(pl.multiple_of(col * block, block), block)].astype(F32)
-    for k in range(1, n_col):
-        sum_copy(k).wait()
-        total = total + landing_ref[k].astype(F32)
+    total = None
+    for k in order:
+        total = sums(k, 0)[...].astype(F32)
+        for m in range(1, inner):
+            near_copy(k, m).wait()
+            total = total + near_ref[k * inner + m].astype(F32)
+        if k > 0:
+            stage_ref[k] = total.astype(BF16)
+            far_copy(k).start()
+    load_first.wait()
+    load_second.wait()
+    base = dot(nodes_ref[...], halved(w1_ref[0]))
+    lower = halved(w1_ref[1])
+    second = centred(w2_ref[...])
+    for k in range(1, outer):
+        far_copy(k).wait()
+        total = total + far_ref[k].astype(F32)
     half = base + dot(total.astype(BF16), lower)
     fresh = scaled(dot(silu_half(half), second), gain_ref[...])
     fresh = (nodes_ref[...].astype(F32) + fresh).astype(BF16)
@@ -261,7 +325,19 @@
 
 
 def grid_kernel(
-    per_peer, grid_ref, index_ref, band_ref, w1_ref, w2_ref, gain_ref, out_ref, first_ref, second_ref, table_ref
+    per_peer,
+    grid_ref,
+    index_ref,
+    band_ref,
+    w1_ref,
+    w2_ref,
+    gain_ref,
+    nodes_ref,
+    out_ref,
+    nodes_out_ref,
+    first_ref,
+    second_ref,
+    table_ref,
 ):
     count = table_ref.shape[0]
     pieces = grid_ref.shape[1] // LANES
@@ -269,6 +345,7 @@
 
     @pl.when(pl.program_id(0) == 0)
     def _():
+        nodes_out_ref[...] = nodes_ref[...]
         first_ref[...] = halved(w1_ref[0])
         second_ref[...] = centred(w2_ref[...])
         shape = (count, count * pieces)
@@ -333,9 +410,9 @@
         out_shape=jax.ShapeDtypeStruct((known, width), BF16),
         in_specs=[VMEM],
         out_specs=VMEM,
-        scratch_shapes=[pltpu.SemaphoreType.DMA((n_row + n_col,)), pltpu.SemaphoreType.DMA((n_row + n_col,))],
+        scratch_shapes=[pltpu.SemaphoreType.DMA((n_row + n_col,))] * 2,
         compiler_params=pltpu.CompilerParams(
-            collective_id=0, has_side_effects=True, vmem_limit_bytes=16 * 2**20
+            collective_id=0, has_side_effects=True, vmem_limit_bytes=VMEM_LIMIT
         ),
         name="gather_nodes",
     )(nodes)
@@ -374,7 +451,7 @@
             pltpu.VMEM((rows, width), BF16),
             pltpu.VMEM((receiver_count, width), F32),
         ],
-        compiler_params=pltpu.CompilerParams(vmem_limit_bytes=44 * 2**20),
+        compiler_params=pltpu.CompilerParams(vmem_limit_bytes=VMEM_LIMIT),
         name="edge_update",
     )(
         counts,
@@ -391,34 +468,45 @@
 
     peers, per_peer = send_rows.shape[1:]
     tile = per_peer * (width // LANES)
-    nodes_out, band = pl.pallas_call(
+    outer = split_of(n_col)[0]
+    fresh_nodes, band = pl.pallas_call(
         functools.partial(node_kernel, n_row, n_col),
         out_shape=(
             jax.ShapeDtypeStruct((block, width), BF16),
             jax.ShapeDtypeStruct((peers * tile, LANES), BF16),
         ),
-        in_specs=[VMEM] * 6,
+        in_specs=[VMEM, VMEM, ANY, ANY, VMEM, VMEM],
         out_specs=(VMEM, VMEM),
         scratch_shapes=[
+            pltpu.VMEM(node_w1.shape, BF16),
+            pltpu.VMEM(node_w2.shape, BF16),
             pltpu.VMEM((n_col, block, width), BF16),
+            pltpu.VMEM((outer, block, width), BF16),
+            pltpu.VMEM((outer, block, width), BF16),
             pltpu.VMEM((peers * tile, LANES), BF16),
+            pltpu.SemaphoreType.DMA((2,)),
             pltpu.SemaphoreType.DMA((n_col,)),
             pltpu.SemaphoreType.DMA((n_col,)),
+            pltpu.SemaphoreType.DMA((outer,)),
+            pltpu.SemaphoreType.DMA((outer,)),
             pltpu.SemaphoreType.DMA((n_dev,)),
             pltpu.SemaphoreType.DMA((n_dev,)),
         ],
         compiler_params=pltpu.CompilerParams(
-            collective_id=1, has_side_effects=True, vmem_limit_bytes=24 * 2**20
+            collective_id=1, has_side_effects=True, vmem_limit_bytes=VMEM_LIMIT
         ),
         name="node_update",
     )(partial, nodes, node_w1, node_w2, node_gain.reshape(1, width), send_rows.reshape(peers, per_peer))
 
     cells, fan = dec_index.shape
     cell_rows = math.gcd(cells, 256)
-    grid_out = pl.pallas_call(
+    grid_out, nodes_out = pl.pallas_call(
         functools.partial(grid_kernel, per_peer),
         grid=(cells // cell_rows,),
-        out_shape=jax.ShapeDtypeStruct((cells, width), BF16),
+        out_shape=(
+            jax.ShapeDtypeStruct((cells, width), BF16),
+            jax.ShapeDtypeStruct((block, width), BF16),
+        ),
         in_specs=[
             pl.BlockSpec((cell_rows, width), lambda i: (i, 0)),
             pl.BlockSpec((fan, cell_rows), lambda i: (0, i)),
@@ -426,16 +514,17 @@
             whole(dec_w1.shape),
             whole(dec_w2.shape),
             whole((1, width)),
+            whole((block, width)),
         ],
-        out_specs=pl.BlockSpec((cell_rows, width), lambda i: (i, 0)),
+        out_specs=(pl.BlockSpec((cell_rows, width), lambda i: (i, 0)), whole((block, width))),
         scratch_shapes=[
             pltpu.VMEM((width, width), BF16),
             pltpu.VMEM((width, width), BF16),
             pltpu.VMEM((peers * per_peer, width), BF16),
         ],
-        compiler_params=pltpu.CompilerParams(vmem_limit_bytes=40 * 2**20),
+        compiler_params=pltpu.CompilerParams(vmem_limit_bytes=VMEM_LIMIT),
         name="grid_update",
-    )(grid, dec_index.T, band, dec_w1, dec_w2, dec_gain.reshape(1, width))
+    )(grid, dec_index.T, band, dec_w1, dec_w2, dec_gain.reshape(1, width), fresh_nodes)
     return (nodes_out, edge_new.reshape(edges.shape), grid_out)
 
 

time: 84.7 us -> 71.8 us (0.85)
  local copies, waits for them, and re-layouts: 13.6 us -> 0.7 us
    unnamed x43 -> x2, local copies, waits for them, and re-layouts: 13.6 us -> 0.01 us
    pallas_call x1, Pallas kernels: 28.8 us -> 23.1 us  [on_device(): pl.pallas_call(functools.partial(node_kernel, n_row, n_col), out_shape=(j...]
    pallas_call x1, Pallas kernels: 16.8 us -> 19.2 us  [on_device(): pl.pallas_call(functools.partial(edge_kernel, sender_count, chunk), grid=...]
    pallas_call x1, Pallas kernels: 15.5 us -> 17.7 us  [on_device(): pl.pallas_call(functools.partial(gather_kernel, n_row, n_col), out_shape=...]
    pallas_call x1, Pallas kernels: 7.84 us -> 9.44 us  [on_device(): pl.pallas_call(functools.partial(grid_kernel, per_peer), grid=(cells // c...]
where the time goes in v2:
time: 71.8 us; the launch traced here: 71.5 us
  Pallas kernels  69.5 us (97%)
  between operations  1.31 us (2%)
    pallas_call x1, Pallas kernels, on_device(): pl.pallas_call(functools.partial(node_kernel, n_row, n_col), out_shape=(j...  23.1 us
    pallas_call x1, Pallas kernels, on_device(): pl.pallas_call(functools.partial(edge_kernel, sender_count, chunk), grid=...  19.2 us
    pallas_call x1, Pallas kernels, on_device(): pl.pallas_call(functools.partial(gather_kernel, n_row, n_col), out_shape=...  17.7 us
    pallas_call x1, Pallas kernels, on_device(): pl.pallas_call(functools.partial(grid_kernel, per_peer), grid=(cells // c...  9.44 us

profile of v2, /device:TPU:0, one launch (start us, length us, event | category | flops | bytes accessed | tf_op | source)
XLA Modules:
  0.0 71.5 jit_solution(1759945424548572482)
XLA Ops:
  0.6 0.0 copy-start
  0.6 17.7 %gather_nodes.1.gathered_ref = bf16[768,512]{1,0:T(8,128)(2,1)} custom-call(bf16[64,512]{1,0:T(8,128)(2,1)} %nodes_ref.3), custom_call_target="tpu_custom_call" | custom-call | tf_op jit(solution)/shard_map/gather_nodes/pallas_call | solution.py:408
  19.0 19.2 %edge_update.1 = (bf16[4096,512]{1,0:T(8,128)(2,1)}, bf16[512,512]{1,0:T(8,128)(2,1)}) custom-call(s32[1,1]{1,0:T(1,128)S(6)} %copy.23.counts_ref, bf16[4096,512]{1,0:T(8,128)(2,1)} %bitcast.10, s32[1,4096]{1,0:T(1,128)} %bitcast.11, s32[1,4096]{1,0:T(1,128)} %bitcast.12, s32[1,4096]{1,0:T(1,128)} %bitcast.13, bf16[768,512]{1,0:T(8,128)(2,1)} %gather_nodes.1.gathered_ref, ...), custom_call_target="tpu_custom_call" | custom-call | tf_op jit(solution)/shard_map/edge_update/pallas_call | solution.py:427
  38.3 0.0 copy-done
  38.3 0.7 copy.22.rows_ref
  39.0 23.1 %node_update.1 = (bf16[64,512]{1,0:T(8,128)(2,1)}, bf16[512,128]{1,0:T(8,128)(2,1)}) custom-call(bf16[512,512]{1,0:T(8,128)(2,1)} %get-tuple-element.9.partial_ref, bf16[64,512]{1,0:T(8,128)(2,1)} %nodes_ref.3, bf16[2,512,512]{2,1,0:T(8,128)(2,1)} %w1_hbm.1, bf16[512,512]{1,0:T(8,128)(2,1)} %w2_hbm.1, f32[1,512]{1,0:T(1,128)} %bitcast.16, s32[32,4]{1,0:T(8,128)} %copy.22.rows_ref), custom_call_target="tpu_custom_call" | custom-call | tf_op jit(solution)/shard_map/node_update/pallas_call | solution.py:472
  62.1 9.4 %grid_update.1 = (bf16[1024,512]{1,0:T(8,128)(2,1)}, bf16[64,512]{1,0:T(8,128)(2,1)}) custom-call(bf16[1024,512]{1,0:T(8,128)(2,1)} %grid_ref.1, s32[3,1024]{1,0:T(4,128)} %bitcast.14, bf16[512,128]{1,0:T(8,128)(2,1)} %get-tuple-element.10.band_ref, bf16[2,512,512]{2,1,0:T(8,128)(2,1)} %w1_ref.3, bf16[512,512]{1,0:T(8,128)(2,1)} %w2_ref.3, ...), custom_call_target="tpu_custom_call" | custom-call | tf_op jit(solution)/shard_map/grid_update/pallas_call | solution.py:503
Async XLA Ops:
  0.6 37.6 %copy-start = (s32[1,32,4]{1,2,0:T(4,128)S(1)}, s32[1,32,4]{1,2,0:T(4,128)}, u32[]{:S(2)}) copy-start(s32[1,32,4]{1,2,0:T(4,128)} %param.33) | copy-start | bytes 1540

commit v3 on v2

--- a/solution.py
+++ b/solution.py
@@ -59,7 +59,29 @@
     return outer, n_col // outer
 
 
-def gather_kernel(n_row, n_col, nodes_ref, out_ref, send_sem, recv_sem):
+def gather_kernel(
+    n_row,
+    n_col,
+    nodes_ref,
+    edges_hbm,
+    levels_ref,
+    w1_hbm,
+    bias_ref,
+    w2_hbm,
+    table_ref,
+    second_ref,
+    own_hbm,
+    out_ref,
+    w1_ref,
+    w2_ref,
+    edges_ref,
+    own_ref,
+    send_sem,
+    recv_sem,
+    weight_sem,
+    load_sem,
+    store_sem,
+):
     row, col = lax.axis_index("row"), lax.axis_index("col")
     outer, inner = split_of(n_col)
     high, low = col // inner, lax.rem(col, inner)
@@ -79,6 +101,20 @@
     friends += [row_dev(k) for k in range(1, n_row)]
     for friend in friends:
         pl.semaphore_signal(barrier, inc=1, device_id=friend, device_id_type=MESH)
+    load_first = pltpu.make_async_copy(w1_hbm, w1_ref, weight_sem.at[0])
+    load_second = pltpu.make_async_copy(w2_hbm, w2_ref, weight_sem.at[1])
+    load_first.start()
+    stages, rows = edges_ref.shape[:2]
+
+    def load(b):
+        return pltpu.make_async_copy(edges_hbm.at[pl.ds(b * rows, rows)], edges_ref.at[b], load_sem.at[b])
+
+    def store(b):
+        return pltpu.make_async_copy(own_ref.at[b], own_hbm.at[pl.ds(b * rows, rows)], store_sem.at[b])
+
+    for b in range(stages):
+        load(b).start()
+    load_second.start()
     pl.semaphore_wait(barrier, len(friends))
 
     def slot(index):
@@ -104,14 +140,40 @@
     own = nodes_ref[...]
     slot(row)[...] = own
     slot(n_row + col)[...] = own
+    load_first.wait()
+    first = halved(w1_ref[0])
+    bias = jnp.concatenate(
+        [halved(bias_ref[...]), jnp.zeros((LANES - bias_ref.shape[0], bias_ref.shape[1]), BF16)], axis=0
+    )
+
+    def own_part(b):
+        load(b).wait()
+        ids = columns_of([levels_ref[:, pl.ds(b * rows, rows)]])
+        own_ref[b] = (dot(edges_ref[b], first) + dot(hot(ids[:, 0:1], LANES), bias)).astype(BF16)
+        store(b).start()
+
+    arrivals = outer - 1
+    for b in range(stages - arrivals if stages > arrivals else 0):
+        own_part(b)
     for k in range(1, outer):
         arrived = copy(nodes_ref, col_slot(k, 0), k * inner, out_dev(k))
         arrived.wait()
         for m in range(1, inner):
             copy(col_slot(k, 0), col_slot(k, 0), k * inner + m, in_dev(m)).start()
             waits.append(copy(col_slot(k, 0), col_slot(k, m), k * inner + m, in_dev(m)))
+        b = stages - outer + k
+        if b >= 0:
+            own_part(b)
+    load_second.wait()
+    second_ref[...] = centred(w2_ref[...])
+    middle, last = halved(w1_ref[1]), halved(w1_ref[2])
     for wait in waits:
         wait.wait()
+    known = n_row * block
+    table_ref[:known] = dot(out_ref[:known], middle).astype(BF16)
+    table_ref[known:] = dot(out_ref[known:], last).astype(BF16)
+    for b in range(stages):
+        store(b).wait()
 
 
 def edge_kernel(
@@ -119,47 +181,35 @@
     chunk,
     counts_ref,
     edges_ref,
+    own_ref,
     senders_ref,
     receivers_ref,
-    levels_ref,
-    gathered_ref,
-    w1_ref,
-    bias_ref,
-    w2_ref,
+    table_ref,
+    second_ref,
     gain_ref,
     edges_out_ref,
     partial_ref,
-    table_ref,
-    first_ref,
-    second_ref,
     message_ref,
     total_ref,
 ):
     step = pl.program_id(0)
     rows = edges_ref.shape[0]
     receiver_count = partial_ref.shape[0]
-    known = sender_count + receiver_count
 
     @pl.when(step == 0)
     def _():
-        first_ref[...] = halved(w1_ref[0])
-        second_ref[...] = centred(w2_ref[...])
-        table_ref[:sender_count] = dot(gathered_ref[:sender_count], halved(w1_ref[1])).astype(BF16)
-        table_ref[sender_count:known] = dot(gathered_ref[sender_count:], halved(w1_ref[2])).astype(BF16)
-        table_ref[known:] = jnp.zeros((table_ref.shape[0] - known, table_ref.shape[1]), BF16)
-        table_ref[known : known + bias_ref.shape[0]] = halved(bias_ref[...])
         total_ref[...] = jnp.zeros_like(total_ref)
 
     count = counts_ref[0, 0]
     gain = gain_ref[...]
     for part in range(rows // chunk):
         span = pl.ds(part * chunk, chunk)
-        ids = columns_of([senders_ref[:, span], receivers_ref[:, span], levels_ref[:, span]])
+        ids = columns_of([senders_ref[:, span], receivers_ref[:, span]])
         chosen = jnp.concatenate(
-            [hot(ids[:, 0:1], sender_count), hot(ids[:, 1:2], receiver_count), hot(ids[:, 2:3], LANES)], axis=1
+            [hot(ids[:, 0:1], sender_count), hot(ids[:, 1:2], receiver_count)], axis=1
         )
         values = edges_ref[span]
-        half = dot(values, first_ref[...]) + dot(chosen, table_ref[...])
+        half = own_ref[span].astype(F32) + dot(chosen, table_ref[...])
         message = scaled(dot(silu_half(half), second_ref[...]), gain).astype(BF16)
         message_ref[span] = message
         place = step * rows + part * chunk + lax.broadcasted_iota(jnp.int32, (chunk, 1), 0)
@@ -207,7 +257,7 @@
     n_dev = n_row * n_col
     block, width = nodes_ref.shape
     pieces = width // LANES
-    per_peer = rows_ref.shape[1]
+    per_peer = rows_ref.shape[0]
     tile = pieces * per_peer
     barrier = pltpu.get_barrier_semaphore()
 
@@ -256,7 +306,12 @@
     count = n_dev * tile
     owner = lax.broadcasted_iota(jnp.int32, (count, n_dev), 0) // tile
     spread = (owner == lax.broadcasted_iota(jnp.int32, (count, n_dev), 1)).astype(F32).astype(BF16)
-    wanted = dot(spread, rows_ref[...].astype(F32).astype(BF16))
+    wanted = lax.dot_general(
+        spread,
+        rows_ref[...].astype(F32).astype(BF16),
+        (((1,), (1,)), ((), ())),
+        preferred_element_type=F32,
+    )
     which = lax.broadcasted_iota(jnp.int32, (count, per_peer), 0) % per_peer
     wanted = jnp.where(which == lax.broadcasted_iota(jnp.int32, (count, per_peer), 1), wanted, 0.0)
     wanted = jnp.sum(wanted, axis=1, keepdims=True)
@@ -405,21 +460,39 @@
     sender_count, receiver_count = block * n_row, block * n_col
     known = sender_count + receiver_count
 
-    gathered = pl.pallas_call(
+    rows = math.gcd(capacity, 1024)
+    chunk = math.gcd(rows, 256)
+    stages = capacity // rows
+    flat = edges.reshape(capacity, width)
+    outer, inner = split_of(n_col)
+    copies = n_row + n_col
+
+    table, second, own = pl.pallas_call(
         functools.partial(gather_kernel, n_row, n_col),
-        out_shape=jax.ShapeDtypeStruct((known, width), BF16),
-        in_specs=[VMEM],
-        out_specs=VMEM,
-        scratch_shapes=[pltpu.SemaphoreType.DMA((n_row + n_col,))] * 2,
+        out_shape=(
+            jax.ShapeDtypeStruct((known, width), BF16),
+            jax.ShapeDtypeStruct((width, width), BF16),
+            jax.ShapeDtypeStruct((capacity, width), BF16),
+        ),
+        in_specs=[VMEM, ANY, VMEM, ANY, VMEM, ANY],
+        out_specs=(VMEM, VMEM, ANY),
+        scratch_shapes=[
+            pltpu.VMEM((known, width), BF16),
+            pltpu.VMEM(edge_w1.shape, BF16),
+            pltpu.VMEM(edge_w2.shape, BF16),
+            pltpu.VMEM((stages, rows, width), BF16),
+            pltpu.VMEM((stages, rows, width), BF16),
+            pltpu.SemaphoreType.DMA((copies,)),
+            pltpu.SemaphoreType.DMA((copies,)),
+            pltpu.SemaphoreType.DMA((2,)),
+            pltpu.SemaphoreType.DMA((stages,)),
+            pltpu.SemaphoreType.DMA((stages,)),
+        ],
         compiler_params=pltpu.CompilerParams(
             collective_id=0, has_side_effects=True, vmem_limit_bytes=VMEM_LIMIT
         ),
         name="gather_nodes",
-    )(nodes)
-
-    rows = math.gcd(capacity, 1024)
-    chunk = math.gcd(rows, 256)
-    table_rows = known + LANES
+    )(nodes, flat, levels.reshape(1, capacity), edge_w1, level_bias, edge_w2)
 
     def id_spec():
         return pl.BlockSpec((1, rows), lambda i: (0, i))
@@ -434,20 +507,15 @@
         in_specs=[
             pl.BlockSpec(memory_space=pltpu.SMEM),
             pl.BlockSpec((rows, width), lambda i: (i, 0)),
-            id_spec(),
+            pl.BlockSpec((rows, width), lambda i: (i, 0)),
             id_spec(),
             id_spec(),
             whole((known, width)),
-            whole(edge_w1.shape),
-            whole(level_bias.shape),
-            whole(edge_w2.shape),
+            whole((width, width)),
             whole((1, width)),
         ],
         out_specs=(pl.BlockSpec((rows, width), lambda i: (i, 0)), whole((receiver_count, width))),
         scratch_shapes=[
-            pltpu.VMEM((table_rows, width), BF16),
-            pltpu.VMEM((width, width), BF16),
-            pltpu.VMEM((width, width), BF16),
             pltpu.VMEM((rows, width), BF16),
             pltpu.VMEM((receiver_count, width), F32),
         ],
@@ -455,20 +523,17 @@
         name="edge_update",
     )(
         counts,
-        edges.reshape(capacity, width),
+        flat,
+        own,
         senders.reshape(1, capacity),
         receivers.reshape(1, capacity),
-        levels.reshape(1, capacity),
-        gathered,
-        edge_w1,
-        level_bias,
-        edge_w2,
+        table,
+        second,
         edge_gain.reshape(1, width),
     )
 
     peers, per_peer = send_rows.shape[1:]
     tile = per_peer * (width // LANES)
-    outer = split_of(n_col)[0]
     fresh_nodes, band = pl.pallas_call(
         functools.partial(node_kernel, n_row, n_col),
         out_shape=(
@@ -496,7 +561,7 @@
             collective_id=1, has_side_effects=True, vmem_limit_bytes=VMEM_LIMIT
         ),
         name="node_update",
-    )(partial, nodes, node_w1, node_w2, node_gain.reshape(1, width), send_rows.reshape(peers, per_peer))
+    )(partial, nodes, node_w1, node_w2, node_gain.reshape(1, width), send_rows[0].T)
 
     cells, fan = dec_index.shape
     cell_rows = math.gcd(cells, 256)

time: 71.8 us -> 68.9 us (0.960)
  Pallas kernels: 69.5 us -> 67.3 us
    pallas_call x1, Pallas kernels: 19.2 us -> 15.4 us  [on_device(): pl.pallas_call(functools.partial(edge_kernel, sender_count, chunk), grid=...]
    pallas_call x1, Pallas kernels: 17.7 us -> 19.3 us  [on_device(): pl.pallas_call(functools.partial(gather_kernel, n_row, n_col), out_shape=...]
where the time goes in v3:
time: 68.9 us; the launch traced here: 68.6 us
  Pallas kernels  67.3 us (98%)
  between operations  1.29 us (2%)
    pallas_call x1, Pallas kernels, on_device(): pl.pallas_call(functools.partial(node_kernel, n_row, n_col), out_shape=(j...  23.2 us
    pallas_call x1, Pallas kernels, on_device(): pl.pallas_call(functools.partial(gather_kernel, n_row, n_col), out_shape=...  19.3 us
    pallas_call x1, Pallas kernels, on_device(): pl.pallas_call(functools.partial(edge_kernel, sender_count, chunk), grid=...  15.4 us
    pallas_call x1, Pallas kernels, on_device(): pl.pallas_call(functools.partial(grid_kernel, per_peer), grid=(cells // c...  9.44 us

profile of v3, /device:TPU:0, one launch (start us, length us, event | category | flops | bytes accessed | tf_op | source)
XLA Modules:
  0.0 68.6 jit_solution(15568565215563922827)
XLA Ops:
  1.3 19.3 %gather_nodes.1 = (bf16[768,512]{1,0:T(8,128)(2,1)}, bf16[512,512]{1,0:T(8,128)(2,1)}, bf16[4096,512]{1,0:T(8,128)(2,1)}) custom-call(bf16[64,512]{1,0:T(8,128)(2,1)} %nodes_ref.3, bf16[4096,512]{1,0:T(8,128)(2,1)} %bitcast.12, s32[1,4096]{1,0:T(1,128)} %bitcast.14, bf16[3,512,512]{2,1,0:T(8,128)(2,1)} %w1_hbm.2, bf16[7,512]{1,0:T(8,128)(2,1)} %bias_ref.1, ...), custom_call_target="tpu_custom_call" | custom-call | tf_op jit(solution)/shard_map/gather_nodes/pallas_call | solution.py:470
  20.6 15.4 %edge_update.1 = (bf16[4096,512]{1,0:T(8,128)(2,1)}, bf16[512,512]{1,0:T(8,128)(2,1)}) custom-call(s32[1,1]{1,0:T(1,128)S(6)} %copy.22.counts_ref, bf16[4096,512]{1,0:T(8,128)(2,1)} %bitcast.13, bf16[4096,512]{1,0:T(8,128)(2,1)} %get-tuple-element.12.own_ref, s32[1,4096]{1,0:T(1,128)} %bitcast.15, s32[1,4096]{1,0:T(1,128)} %bitcast.16, ...), custom_call_target="tpu_custom_call" | custom-call | tf_op jit(solution)/shard_map/edge_update/pallas_call | solution.py:500
  36.0 23.2 %node_update.1 = (bf16[64,512]{1,0:T(8,128)(2,1)}, bf16[512,128]{1,0:T(8,128)(2,1)}) custom-call(bf16[512,512]{1,0:T(8,128)(2,1)} %get-tuple-element.15.partial_ref, bf16[64,512]{1,0:T(8,128)(2,1)} %nodes_ref.3, bf16[2,512,512]{2,1,0:T(8,128)(2,1)} %w1_hbm.3, bf16[512,512]{1,0:T(8,128)(2,1)} %w2_hbm.3, f32[1,512]{1,0:T(1,128)} %bitcast.19, s32[4,32]{1,0:T(4,128)} %bitcast.20), custom_call_target="tpu_custom_call" | custom-call | tf_op jit(solution)/shard_map/node_update/pallas_call | solution.py:537
  59.2 9.4 %grid_update.1 = (bf16[1024,512]{1,0:T(8,128)(2,1)}, bf16[64,512]{1,0:T(8,128)(2,1)}) custom-call(bf16[1024,512]{1,0:T(8,128)(2,1)} %grid_ref.1, s32[3,1024]{1,0:T(4,128)} %bitcast.17, bf16[512,128]{1,0:T(8,128)(2,1)} %get-tuple-element.16.band_ref, bf16[2,512,512]{2,1,0:T(8,128)(2,1)} %w1_ref.1, bf16[512,512]{1,0:T(8,128)(2,1)} %w2_ref.1, ...), custom_call_target="tpu_custom_call" | custom-call | tf_op jit(solution)/shard_map/grid_update/pallas_call | solution.py:568

commit v4 on v3

--- a/solution.py
+++ b/solution.py
@@ -564,7 +564,7 @@
     )(partial, nodes, node_w1, node_w2, node_gain.reshape(1, width), send_rows[0].T)
 
     cells, fan = dec_index.shape
-    cell_rows = math.gcd(cells, 256)
+    cell_rows = math.gcd(cells, 512)
     grid_out, nodes_out = pl.pallas_call(
         functools.partial(grid_kernel, per_peer),
         grid=(cells // cell_rows,),

time: 68.9 us -> 67.1 us (0.974)
  Pallas kernels: 67.3 us -> 65.6 us
    pallas_call x1, Pallas kernels: 9.44 us -> 7.66 us  [on_device(): pl.pallas_call(functools.partial(grid_kernel, per_peer), grid=(cells // c...]
where the time goes in v4:
time: 67.1 us; the launch traced here: 66.9 us
  Pallas kernels  65.6 us (98%)
  between operations  1.29 us (2%)
    pallas_call x1, Pallas kernels, on_device(): pl.pallas_call(functools.partial(node_kernel, n_row, n_col), out_shape=(j...  23.2 us
    pallas_call x1, Pallas kernels, on_device(): pl.pallas_call(functools.partial(gather_kernel, n_row, n_col), out_shape=...  19.3 us
    pallas_call x1, Pallas kernels, on_device(): pl.pallas_call(functools.partial(edge_kernel, sender_count, chunk), grid=...  15.4 us
    pallas_call x1, Pallas kernels, on_device(): pl.pallas_call(functools.partial(grid_kernel, per_peer), grid=(cells // c...  7.66 us

profile of v4, /device:TPU:0, one launch (start us, length us, event | category | flops | bytes accessed | tf_op | source)
XLA Modules:
  0.0 66.9 jit_solution(3277312609183235943)
XLA Ops:
  1.3 19.3 %gather_nodes.1 = (bf16[768,512]{1,0:T(8,128)(2,1)}, bf16[512,512]{1,0:T(8,128)(2,1)}, bf16[4096,512]{1,0:T(8,128)(2,1)}) custom-call(bf16[64,512]{1,0:T(8,128)(2,1)} %nodes_ref.3, bf16[4096,512]{1,0:T(8,128)(2,1)} %bitcast.12, s32[1,4096]{1,0:T(1,128)} %bitcast.14, bf16[3,512,512]{2,1,0:T(8,128)(2,1)} %w1_hbm.2, bf16[7,512]{1,0:T(8,128)(2,1)} %bias_ref.1, ...), custom_call_target="tpu_custom_call" | custom-call | tf_op jit(solution)/shard_map/gather_nodes/pallas_call | solution.py:470
  20.6 15.4 %edge_update.1 = (bf16[4096,512]{1,0:T(8,128)(2,1)}, bf16[512,512]{1,0:T(8,128)(2,1)}) custom-call(s32[1,1]{1,0:T(1,128)S(6)} %copy.22.counts_ref, bf16[4096,512]{1,0:T(8,128)(2,1)} %bitcast.13, bf16[4096,512]{1,0:T(8,128)(2,1)} %get-tuple-element.12.own_ref, s32[1,4096]{1,0:T(1,128)} %bitcast.15, s32[1,4096]{1,0:T(1,128)} %bitcast.16, ...), custom_call_target="tpu_custom_call" | custom-call | tf_op jit(solution)/shard_map/edge_update/pallas_call | solution.py:500
  36.0 23.2 %node_update.1 = (bf16[64,512]{1,0:T(8,128)(2,1)}, bf16[512,128]{1,0:T(8,128)(2,1)}) custom-call(bf16[512,512]{1,0:T(8,128)(2,1)} %get-tuple-element.15.partial_ref, bf16[64,512]{1,0:T(8,128)(2,1)} %nodes_ref.3, bf16[2,512,512]{2,1,0:T(8,128)(2,1)} %w1_hbm.3, bf16[512,512]{1,0:T(8,128)(2,1)} %w2_hbm.3, f32[1,512]{1,0:T(1,128)} %bitcast.19, s32[4,32]{1,0:T(4,128)} %bitcast.20), custom_call_target="tpu_custom_call" | custom-call | tf_op jit(solution)/shard_map/node_update/pallas_call | solution.py:537
  59.2 7.7 %grid_update.1 = (bf16[1024,512]{1,0:T(8,128)(2,1)}, bf16[64,512]{1,0:T(8,128)(2,1)}) custom-call(bf16[1024,512]{1,0:T(8,128)(2,1)} %grid_ref.1, s32[3,1024]{1,0:T(4,128)} %bitcast.17, bf16[512,128]{1,0:T(8,128)(2,1)} %get-tuple-element.16.band_ref, bf16[2,512,512]{2,1,0:T(8,128)(2,1)} %w1_ref.1, bf16[512,512]{1,0:T(8,128)(2,1)} %w2_ref.1, ...), custom_call_target="tpu_custom_call" | custom-call | tf_op jit(solution)/shard_map/grid_update/pallas_call | solution.py:568
